TPU v7x, 128 devices: a whole 4x4x4 slice. The times are simulated.
128 devices in a mesh: tp: 16 (over x, z_lo, core), dp: 8 (over y, z_hi).
Axes of the slice: x: 4, y: 4, z: 4 (z_hi: 2, z_lo: 2; z = z_hi * 2 + z_lo), core: 2. Of those that a mesh axis runs over, the one named last changes fastest.
Arguments:
- grad_out: bfloat16 [7168, 8192], P(('dp', 'tp')), may hold values from -6 to 6
- gate_act: bfloat16 [7168, 14336], P('dp', 'tp'), may hold values from -8 to 8
- up_act: bfloat16 [7168, 14336], P('dp', 'tp'), may hold values from -6 to 6
- down_weight: bfloat16 [14336, 8192], P('tp'), may hold values from -0.0625 to 0.0625
Outputs:
- grad_gate: bfloat16 [7168, 14336], P('dp', 'tp')
- grad_up: bfloat16 [7168, 14336], P('dp', 'tp')
- grad_down: bfloat16 [14336, 8192], P(('tp', 'dp'))
All inputs are finite; a program needn't handle non-finite values.
Results may differ from a plain program's by a relative error of at most 0.013.
Values may be sent and summed in bfloat16 or wider, within the bound.
A program may use at most 128 MiB of HBM per device.

v0:
```python
import math

import jax
import jax.numpy as jnp
from jax import lax
from jax.sharding import PartitionSpec as P


def body(grad_out, gate_act, up_act, down_weight):
    gate_val = gate_act.astype(jnp.float32)
    up_val = up_act.astype(jnp.float32)
    squash = jax.nn.sigmoid(gate_val)
    hidden = (gate_val * squash * up_val).astype(jnp.bfloat16)
    incoming = lax.all_gather(grad_out, "tp", axis=0, tiled=True)
    row_store = incoming
    new_rows = lax.dot_general(
        incoming, down_weight, (((1,), (1,)), ((), ())), preferred_element_type=jnp.float32
    )
    row_store, grad_hidden = (row_store, new_rows)
    weight_part = lax.dot_general(
        hidden, row_store, (((0,), (0,)), ((), ())), preferred_element_type=jnp.float32
    )
    summed = lax.psum_scatter(
        weight_part.astype(jnp.bfloat16), "dp", scatter_dimension=0, tiled=True
    ).astype(jnp.float32)
    grad_gate = (grad_hidden * up_val * squash * (1.0 + gate_val * (1.0 - squash))).astype(
        jnp.bfloat16
    )
    grad_up = (grad_hidden * gate_val * squash).astype(jnp.bfloat16)
    token_total = grad_out.shape[0] * lax.axis_size("tp") * lax.axis_size("dp")
    grad_scale = 1.0 / math.sqrt(token_total)
    grad_down = (summed * grad_scale).astype(jnp.bfloat16)
    return (grad_gate, grad_up, grad_down)


def solution(mesh):
    return jax.shard_map(
        body,
        mesh=mesh,
        in_specs=(P(("dp", "tp"), None), P("dp", "tp"), P("dp", "tp"), P("tp", None)),
        out_specs=(P("dp", "tp"), P("dp", "tp"), P(("tp", "dp"), None)),
        check_vma=False,
    )
```

profile of v0, /device:TPU:0, one launch (start us, length us, event | category | flops | bytes accessed | tf_op | source)
XLA Modules:
  0.0 298.4 jit_solution(16724781172548772082)
XLA Ops:
  7.2 0.0 all-gather.2.cloned.1.call-start
  7.2 0.7 all-gather.2.cloned.1.call-update
  7.9 0.0 reduce-scatter.2.cloned.1.call-start
  7.9 86.0 %all-gather.2.cloned.1.call-done = bf16[896,8192]{1,0:T(8,128)(2,1)} async-done(((bf16[56,8192]{1,0:T(8,128)(2,1)}), bf16[896,8192]{1,0:T(8,128)(2,1)}) %all-gather.2.cloned.1.call-update) | async-done | bytes 14680080 | tf_op jit(solution)/shard_map/all_gather | solution.py:14
  94.0 23.0 %convolution_convert_fusion = bf16[896,8192]{1,0:T(8,128)(2,1)} fusion(bf16[896,8192]{1,0:T(8,128)(2,1)} %all-gather.2.cloned.1.call-done, bf16[896,896]{1,0:T(8,128)(2,1)} %param.6, bf16[896,896]{1,0:T(8,128)(2,1)} %param.5), kind=kOutput, calls=%fused_computation | convolution fusion | flops 13167099904 | bytes 32571392 | tf_op jit(solution)/shard_map/dot_general | solution.py:20
  117.0 0.0 copy-start
  117.0 0.0 copy-start.1
  117.0 0.0 reduce-scatter.2.cloned.1.call-update
  117.0 1.4 copy-done
  118.4 0.5 copy-done.1
  118.9 26.6 %fusion.9 = (bf16[896,896]{1,0:T(8,128)(2,1)}, bf16[896,896]{1,0:T(8,128)(2,1)}) fusion(bf16[896,896]{1,0:T(8,128)(2,1)S(1)} %copy-done, bf16[896,896]{1,0:T(8,128)(2,1)S(1)} %copy-done.1, bf16[896,8192]{1,0:T(8,128)(2,1)} %all-gather.2.cloned.1.call-done, bf16[896,8192]{1,0:T(8,128)(2,1)} %param.7), kind=kOutput, calls=%fused_computation.17 | convolution fusion | flops 13165379584 | bytes 35782656 | tf_op jit(solution)/shard_map/dot_general | solution.py:16
  145.5 143.0 %reduce-scatter.2.cloned.1.call-done = bf16[112,8192]{1,0:T(8,128)(2,1)} async-done(((bf16[896,8192]{1,0:T(8,128)(2,1)}), bf16[112,8192]{1,0:T(8,128)(2,1)}) %reduce-scatter.2.cloned.1.call-update) | async-done | bytes 1835024 | tf_op jit(solution)/shard_map/reduce_scatter | solution.py:23
  288.5 3.1 %multiply_convert_fusion = bf16[112,8192]{1,0:T(8,128)(2,1)} fusion(bf16[112,8192]{1,0:T(8,128)(2,1)} %reduce-scatter.2.cloned.1.call-done), kind=kLoop, calls=%fused_computation.7 | loop fusion | flops 2752512 | bytes 3670016 | tf_op jit(solution)/shard_map/convert_element_type | solution.py:32
Async XLA Ops:
  7.2 86.8 %all-gather.2.cloned.1.call-start = ((), (), s32[]{:S(2)}) async-start(), calls=%async_computation.1 | async-start | bytes 15597568 | tf_op jit(solution)/shard_map/all_gather | solution.py:14
  7.9 280.6 %reduce-scatter.2.cloned.1.call-start = ((), (), s32[]{:S(2)}) async-start(), calls=%async_computation.2 | async-start | bytes 16515072 | tf_op jit(solution)/shard_map/reduce_scatter | solution.py:23
  117.0 1.4 copy-start
  117.0 1.9 copy-start.1
Sparse Core Ops, SparseCore 0:
  9.7 84.2 all-gather.1
  117.1 171.3 reduce-scatter.1
where the time goes:
time: 299 us; the launch traced here: 298 us
  waiting for transfers between devices  230 us (77%)
  matrix products  49.6 us (17%)
  between operations  14 us (5%)
  other arithmetic  3.07 us (1%)
    reduce_scatter x1, waiting for transfers between devices, body(): lax.psum_scatter(weight_part.astype(jnp.bfloat16), 'dp', scatter_dimensio...  143 us
    all_gather x1, waiting for transfers between devices, body(): incoming = lax.all_gather(grad_out, 'tp', axis=0, tiled=True)  86 us
    dot_general x1, matrix products, body(): lax.dot_general(incoming, down_weight, (((1,), (1,)), ((), ())), preferre...  26.6 us
    dot_general x1, matrix products, body(): lax.dot_general(hidden, row_store, (((0,), (0,)), ((), ())), preferred_el...  23 us
  transfers between devices with their start and end apart: 2, of which 2 were waited for; matrix products, arithmetic and copies ran while one was open for 9% of the time, Pallas kernels for 0%

commit v1 on v0

v1 whole, which is shorter than its diff:
```python
import functools
import math

import jax
import jax.numpy as jnp
from jax import lax
from jax.experimental import pallas as pl
from jax.experimental.pallas import tpu as pltpu
from jax.sharding import PartitionSpec as P

MESH = pl.DeviceIdType.MESH
D = 8192
FF = 896
GROUP = 896
CHUNK = 112
SLICES = 16
W = D // 2 // SLICES
HALF = D // 2
MSGS = 15
BLK = 128
DEPTH = 8


def kernel(scale, go_ref, gate_ref, up_ref, w_ref, gg_ref, gu_ref, gd_ref,
           g, ht, ho, gate, up, acc, wbuf, part, ra, rb, rc, mine, theirs, gd,
           ss, rs, hs, hr, ls, lr, wsem, lsem, osem):
    tp, dp = lax.axis_index("tp"), lax.axis_index("dp")
    x, y, c = tp // 4, dp // 2, tp % 2
    zh, zl = dp % 2, (tp // 2) % 2
    z = zh * 2 + zl
    f32 = jnp.float32

    def at(xx, yy, zz, cc):
        return {"dp": yy * 2 + zz // 2, "tp": xx * 4 + (zz % 2) * 2 + cc}

    def kind(k):
        return jnp.where((k % 2 == 0) & (k >= 2), 1, 0)

    def pq(k):
        b = kind(k)
        return x + b * (z - x), z + b * (x - z)

    def q_dev(k, d):
        b = kind(k)
        return at((x + b * d + 4) % 4, y, (z + (1 - b) * d + 4) % 4, c)

    def p_dev(k, d):
        b = kind(k)
        return at((x + (1 - b) * d + 4) % 4, y, (z + b * d + 4) % 4, c)

    def y_dev(d):
        return at(x, (y + d + 4) % 4, z, c)

    sib = at(x, y, z, 1 - c)
    partner = at(x, y, (z + 2) % 4, c)

    def rcopy(ref, k, m, dev):
        return pltpu.make_async_remote_copy(
            src_ref=ref, dst_ref=ref, send_sem=ss.at[k, m], recv_sem=rs.at[k, m],
            device_id=dev, device_id_type=MESH)

    def one(h, k, p, q):
        return g.at[h, k, pl.ds(((p + 4) % 4) * 4 + (q + 4) % 4, 1)]

    def group(h, k, p):
        return g.at[h, k, pl.ds(((p + 4) % 4) * 4, 4)]

    def half(h, k, p, j):
        return g.at[h, k, pl.ds(((p + 4) % 4) * 4 + 2 * j, 2)]

    def sgn(k):
        return 1 - 2 * ((k // 2) % 2)

    def ysgn(k):
        return 1 - 2 * (k % 2)

    cp_gate = pltpu.make_async_copy(gate_ref, gate, lsem.at[0])
    cp_up = pltpu.make_async_copy(up_ref, up, lsem.at[1])
    cp_mine = pltpu.make_async_copy(go_ref.at[:, pl.ds(pl.multiple_of(c * HALF, HALF), HALF)], mine, lsem.at[2])
    cp_mine.start()
    cp_gate.start()
    cp_up.start()

    barrier = pltpu.get_barrier_semaphore()
    for dev in (at((x + 1) % 4, y, z, c), at((x + 3) % 4, y, z, c), at(x, y, (z + 1) % 4, c),
                at(x, y, (z + 3) % 4, c), y_dev(1), y_dev(-1), sib, partner):
        pl.semaphore_signal(barrier, inc=1, device_id=dev, device_id_type=MESH)
    pl.semaphore_wait(barrier, 8)

    cp_sib = pltpu.make_async_remote_copy(
        src_ref=go_ref.at[:, pl.ds(pl.multiple_of((1 - c) * HALF, HALF), HALF)], dst_ref=theirs,
        send_sem=ls.at[0], recv_sem=lr.at[0], device_id=sib, device_id_type=MESH)
    cp_sib.start()
    acc[...] = jnp.zeros_like(acc)
    cp_mine.wait()
    cp_sib.wait()

    cp_hid = pltpu.make_async_remote_copy(
        src_ref=ht.at[:, 1 - zh], dst_ref=ho, send_sem=hs.at[0], recv_sem=hr.at[0],
        device_id=partner, device_id_type=MESH)

    def w_copy(k, h):
        cols = pl.ds(pl.multiple_of(h * HALF + k * W, W), W)
        return pltpu.make_async_copy(w_ref.at[:, cols], wbuf.at[k % 3, h], wsem.at[k % 3, h])

    def e1(k):
        p, q = pq(k)
        cols = pl.ds(pl.multiple_of(k * W, W), W)
        a, b = mine[:, cols], theirs[:, cols]
        first, last = jnp.where(c == 0, a, b), jnp.where(c == 0, b, a)
        g[c, k, p * 4 + q] = jnp.concatenate([first, last], axis=0)
        rcopy(one(c, k, p, q), k, 0, q_dev(k, 1)).start()
        rcopy(one(c, k, p, q), k, 1, q_dev(k, -1)).start()

    def e2(k):
        p, q = pq(k)
        rcopy(one(c, k, p, q - 1), k, 0, q_dev(k, 1)).wait_recv()
        rcopy(one(c, k, p, q + 1), k, 1, q_dev(k, 1)).wait_recv()
        s = sgn(k)
        rcopy(one(c, k, p, q - s), k, 2, q_dev(k, s)).start()

    def e3(k):
        p, q = pq(k)
        rcopy(one(c, k, p, q + 2), k, 2, q_dev(k, 1)).wait_recv()
        rcopy(group(c, k, p), k, 3, p_dev(k, 1)).start()
        rcopy(group(c, k, p), k, 4, p_dev(k, -1)).start()
        rcopy(group(c, k, p), k, 7, sib).start()

    def e4(k):
        p, q = pq(k)
        rcopy(group(c, k, p - 1), k, 3, p_dev(k, 1)).wait_recv()
        rcopy(half(c, k, p - 1, 0), k, 5, p_dev(k, 1)).start()
        rcopy(group(c, k, p - 1), k, 8, sib).start()
        rcopy(group(c, k, p + 1), k, 4, p_dev(k, 1)).wait_recv()
        rcopy(half(c, k, p + 1, 1), k, 6, p_dev(k, -1)).start()
        rcopy(group(c, k, p + 1), k, 9, sib).start()
        for h in range(2):
            w_copy(k, h).start()

    def e5(k):
        p, q = pq(k)
        rcopy(half(c, k, p + 2, 0), k, 5, p_dev(k, 1)).wait_recv()
        rcopy(half(c, k, p + 2, 0), k, 10, sib).start()
        rcopy(half(c, k, p + 2, 1), k, 6, p_dev(k, 1)).wait_recv()
        rcopy(half(c, k, p + 2, 1), k, 11, sib).start()

    def rows(h, k, zz):
        b = kind(k)
        blocks = []
        for j in range(8):
            xj, zj = j // 2, zz * 2 + j % 2
            pos = (1 - b) * (xj * 4 + zj) + b * (zj * 4 + xj)
            blocks.append(g[h, k, pos])
        return jnp.concatenate(blocks, axis=0)

    def y_copy(k, src, dst, m, d):
        return pltpu.make_async_remote_copy(
            src_ref=src, dst_ref=dst, send_sem=ss.at[k, m], recv_sem=rs.at[k, m],
            device_id=y_dev(d), device_id_type=MESH)

    def blk(k, d):
        return part.at[k, (y + d + 4) % 4]

    def e6(k):
        p, q = pq(k)
        rcopy(group(1 - c, k, p), k, 7, sib).wait_recv()
        rcopy(group(1 - c, k, p - 1), k, 8, sib).wait_recv()
        rcopy(group(1 - c, k, p + 1), k, 9, sib).wait_recv()
        rcopy(half(1 - c, k, p + 2, 0), k, 10, sib).wait_recv()
        rcopy(half(1 - c, k, p + 2, 1), k, 11, sib).wait_recv()
        for h in range(2):
            own = ht[:, zh].reshape(FF // 2, GROUP)
            dw = jnp.dot(own, rows(h, k, zh), preferred_element_type=f32)
            dw += jnp.dot(ho[...].reshape(FF // 2, GROUP), rows(h, k, 1 - zh), preferred_element_type=f32)
            part[k, :, :, h * W:(h + 1) * W] = dw.astype(jnp.bfloat16).reshape(4, CHUNK, W)
        s = ysgn(k)
        y_copy(k, blk(k, 2), ra.at[k], 12, s).start()
        y_copy(k, blk(k, -s), rc.at[k], 14, -s).start()

    def e6b(k):
        for h in range(2):
            w_copy(k, h).wait()
        total = acc[...]
        for h in range(2):
            total += lax.dot_general(rows(h, k, zh), wbuf[k % 3, h], (((1,), (1,)), ((), ())),
                                     preferred_element_type=f32)
        acc[...] = total

    def e7(k):
        s = ysgn(k)
        y_copy(k, blk(k, 2), ra.at[k], 12, s).wait_recv()
        mid = (y + s + 4) % 4
        part[k, mid] = (part[k, mid].astype(f32) + ra[k].astype(f32)).astype(jnp.bfloat16)
        y_copy(k, blk(k, s), rb.at[k], 13, s).start()

    def e8(k):
        s = ysgn(k)
        p, q = pq(k)
        y_copy(k, blk(k, s), rb.at[k], 13, s).wait_recv()
        y_copy(k, blk(k, -s), rc.at[k], 14, -s).wait_recv()
        total = part[k, y].astype(f32) + rb[k].astype(f32) + rc[k].astype(f32)
        total = (total * scale).astype(jnp.bfloat16)
        for h in range(2):
            gd[:, pl.ds(pl.multiple_of(h * HALF + k * W, W), W)] = total[:, h * W:(h + 1) * W]
        rcopy(one(c, k, p, q), k, 0, sib).wait_send()
        rcopy(one(c, k, p, q), k, 1, sib).wait_send()
        rcopy(one(c, k, p, q - sgn(k)), k, 2, sib).wait_send()
        rcopy(group(c, k, p), k, 3, sib).wait_send()
        rcopy(group(c, k, p), k, 4, sib).wait_send()
        rcopy(half(c, k, p - 1, 0), k, 5, sib).wait_send()
        rcopy(half(c, k, p + 1, 1), k, 6, sib).wait_send()
        rcopy(group(c, k, p), k, 7, sib).wait_send()
        rcopy(group(c, k, p - 1), k, 8, sib).wait_send()
        rcopy(group(c, k, p + 1), k, 9, sib).wait_send()
        rcopy(half(c, k, p + 2, 0), k, 10, sib).wait_send()
        rcopy(half(c, k, p + 2, 1), k, 11, sib).wait_send()
        y_copy(k, blk(k, 2), ra.at[k], 12, s).wait_send()
        y_copy(k, blk(k, s), rb.at[k], 13, s).wait_send()
        y_copy(k, blk(k, -s), rc.at[k], 14, -s).wait_send()

    def hidden_block(t):
        at_t = pl.ds(pl.multiple_of(t * BLK, BLK), BLK)
        gv, uv = gate[at_t, :].astype(f32), up[at_t, :].astype(f32)
        hid = (gv * jax.nn.sigmoid(gv) * uv).T.astype(jnp.bfloat16)
        ht[:, :, :, at_t] = hid.reshape(4, 2, CHUNK, BLK)

    def step(i, carry):
        def stage(off, fn):
            k = i - off

            @pl.when((k >= 0) & (k < SLICES))
            def _():
                fn(k)

        stage(2, e3)
        stage(1, e2)
        stage(0, e1)

        @pl.when(i == 0)
        def _():
            cp_gate.wait()
            cp_up.wait()

        @pl.when(i < 4)
        def _():
            hidden_block(2 * i)

        @pl.when(i < 3)
        def _():
            hidden_block(2 * i + 1)

        @pl.when(i == 3)
        def _():
            cp_hid.start()

        stage(4, e4)
        stage(5, e5)

        @pl.when(i == 6)
        def _():
            cp_hid.wait()

        stage(6, e6)
        stage(7, e7)
        stage(6, e6b)
        stage(8, e8)
        return carry

    lax.fori_loop(0, SLICES + DEPTH, step, 0)

    cp_gd = pltpu.make_async_copy(gd, gd_ref, osem.at[0])
    cp_gd.start()

    def finish(t, carry):
        at_t = pl.ds(pl.multiple_of(t * BLK, BLK), BLK)
        gv, uv, gh = gate[at_t, :].astype(f32), up[at_t, :].astype(f32), acc[at_t, :]
        sq = jax.nn.sigmoid(gv)
        gate[at_t, :] = (gh * uv * sq * (1.0 + gv * (1.0 - sq))).astype(jnp.bfloat16)
        up[at_t, :] = (gh * gv * sq).astype(jnp.bfloat16)
        return carry

    lax.fori_loop(0, GROUP // BLK, finish, 0)
    cp_gg = pltpu.make_async_copy(gate, gg_ref, osem.at[1])
    cp_gu = pltpu.make_async_copy(up, gu_ref, osem.at[2])
    cp_gg.start()
    cp_gu.start()
    cp_gd.wait()
    cp_gg.wait()
    cp_gu.wait()


def body(grad_out, gate_act, up_act, down_weight):
    token_total = grad_out.shape[0] * lax.axis_size("tp") * lax.axis_size("dp")
    bf16 = jnp.bfloat16
    any_spec = pl.BlockSpec(memory_space=pl.ANY)
    dma = pltpu.SemaphoreType.DMA
    return pl.pallas_call(
        functools.partial(kernel, 1.0 / math.sqrt(token_total)),
        out_shape=(jax.ShapeDtypeStruct((GROUP, FF), bf16), jax.ShapeDtypeStruct((GROUP, FF), bf16),
                   jax.ShapeDtypeStruct((CHUNK, D), bf16)),
        in_specs=[any_spec] * 4,
        out_specs=(any_spec,) * 3,
        scratch_shapes=[
            pltpu.VMEM((2, SLICES, 16, CHUNK, W), bf16),
            pltpu.VMEM((4, 2, CHUNK, GROUP), bf16),
            pltpu.VMEM((4, CHUNK, GROUP), bf16),
            pltpu.VMEM((GROUP, FF), bf16),
            pltpu.VMEM((GROUP, FF), bf16),
            pltpu.VMEM((GROUP, FF), jnp.float32),
            pltpu.VMEM((3, 2, FF, W), bf16),
            pltpu.VMEM((SLICES, 4, CHUNK, 2 * W), bf16),
            pltpu.VMEM((SLICES, CHUNK, 2 * W), bf16),
            pltpu.VMEM((SLICES, CHUNK, 2 * W), bf16),
            pltpu.VMEM((SLICES, CHUNK, 2 * W), bf16),
            pltpu.VMEM((CHUNK // 2, HALF), bf16),
            pltpu.VMEM((CHUNK // 2, HALF), bf16),
            pltpu.VMEM((CHUNK, D), bf16),
            dma((SLICES, MSGS)), dma((SLICES, MSGS)),
            dma((1,)), dma((1,)), dma((1,)), dma((1,)),
            dma((3, 2)), dma((3,)), dma((3,)),
        ],
        compiler_params=pltpu.CompilerParams(
            collective_id=0, has_side_effects=True, vmem_limit_bytes=62 * 1024 * 1024),
        cost_estimate=pl.CostEstimate(flops=4 * FF * GROUP * D, bytes_accessed=24 * 1024 * 1024,
                                      transcendentals=GROUP * FF * 2),
    )(grad_out, gate_act, up_act, down_weight)


def solution(mesh):
    return jax.shard_map(
        body,
        mesh=mesh,
        in_specs=(P(("dp", "tp"), None), P("dp", "tp"), P("dp", "tp"), P("tp", None)),
        out_specs=(P("dp", "tp"), P("dp", "tp"), P(("tp", "dp"), None)),
        check_vma=False,
    )
```

time: 299 us -> 169 us (0.57)
  waiting for transfers between devices: 230 us -> 0 us
  Pallas kernels: 0 us -> 162 us
  matrix products: 49.6 us -> 0 us
  between operations: 14 us -> 0.65 us
  local copies, waits for them, and re-layouts: 1.88 us -> 6.13 us
  other arithmetic: 3.07 us -> 0 us
    pallas_call x0 -> x1, Pallas kernels: none -> 162 us  [body(): pl.pallas_call(functools.partial(kernel, 1.0 / math.sqrt(token_total)), o...]
    reduce_scatter x1 -> x0, waiting for transfers between devices: 143 us -> none  [body(): lax.psum_scatter(weight_part.astype(jnp.bfloat16), 'dp', scatter_dimensio...]
    all_gather x1 -> x0, waiting for transfers between devices: 86 us -> none  [body(): incoming = lax.all_gather(grad_out, 'tp', axis=0, tiled=True)]
    dot_general x2 -> x0, matrix products: 49.6 us -> none  [the longest x1 26.6 us: body(): lax.dot_general(incoming, down_weight, (((1,), (1,)), ((), ())), preferre...]
    unnamed x4 -> x7, local copies, waits for them, and re-layouts: 1.88 us -> 6.13 us
    convert_element_type x1 -> x0, other arithmetic: 3.07 us -> none  [body(): grad_down = (summed * grad_scale).astype(jnp.bfloat16)]
  transfers between devices with their start and end apart: 2 -> 0, of which waited for: 2 -> 0; matrix products, arithmetic and copies ran while one was open for 9% -> 0% of each run, Pallas kernels for 0% -> 0%
where the time goes in v1:
time: 169 us; the launch traced here: 168 us
  Pallas kernels  162 us (96%)
  local copies, waits for them, and re-layouts  6.13 us (4%)
    pallas_call x1, Pallas kernels, body(): pl.pallas_call(functools.partial(kernel, 1.0 / math.sqrt(token_total)), o...  162 us
    unnamed x7, local copies, waits for them, and re-layouts  6.13 us

profile of v1, /device:TPU:0, one launch (start us, length us, event | category | flops | bytes accessed | tf_op | source)
XLA Modules:
  0.0 168.4 jit_solution(16895798132247290981)
XLA Ops:
  0.6 161.6 %shard_map.67 = (bf16[896,896]{1,0:T(8,128)(2,1)}, bf16[896,896]{1,0:T(8,128)(2,1)}, bf16[112,8192]{1,0:T(8,128)(2,1)}) custom-call(bf16[56,8192]{1,0:T(8,128)(2,1)} %go_ref.1, bf16[896,896]{1,0:T(8,128)(2,1)} %gate_ref.1, bf16[896,896]{1,0:T(8,128)(2,1)} %up_ref.1, bf16[896,8192]{1,0:T(8,128)(2,1)} %w_ref.1), custom_call_target="tpu_custom_call" | custom-call | flops 26306674688 | bytes 25165824 | tf_op jit(solution)/shard_map/pallas_call | solution.py:297
  162.2 0.0 copy-start.1
  162.2 2.8 %copy.10 = bf16[896,896]{1,0:T(8,128)(2,1)} copy(bf16[896,896]{1,0:T(8,128)(2,1)} %get-tuple-element.6) | data formatting | bytes 3211264
  165.1 0.0 copy-done.1
  165.1 0.0 copy-start
  165.1 1.2 copy.11
  166.2 0.9 copy-done
  167.1 1.2 copy.12
Async XLA Ops:
  162.2 2.8 %copy-start.1 = (bf16[896,896]{1,0:T(8,128)(2,1)S(1)}, bf16[896,896]{1,0:T(8,128)(2,1)}, u32[]{:S(2)}) copy-start(bf16[896,896]{1,0:T(8,128)(2,1)} %get-tuple-element.7) | copy-start | bytes 4816900
  165.1 2.1 %copy-start = (bf16[112,8192]{1,0:T(8,128)(2,1)S(1)}, bf16[112,8192]{1,0:T(8,128)(2,1)}, u32[]{:S(2)}) copy-start(bf16[112,8192]{1,0:T(8,128)(2,1)} %get-tuple-element.8) | copy-start | bytes 5505028

commit v2 on v1

--- a/solution.py
+++ b/solution.py
@@ -14,11 +14,15 @@
 GROUP = 896
 CHUNK = 112
 SLICES = 16
+TAIL = 2
 W = D // 2 // SLICES
 HALF = D // 2
 MSGS = 15
 BLK = 128
-DEPTH = 8
+BLOCKS = GROUP // BLK
+HID_PER = 1
+FIN_PER = 3
+O1, O2, O3, O4, O5, O6, O6B, O7, O8 = 0, 2, 4, 6, 8, 9, 9, 10, 11
 
 
 def kernel(scale, go_ref, gate_ref, up_ref, w_ref, gg_ref, gu_ref, gd_ref,
@@ -83,9 +87,9 @@
 
     barrier = pltpu.get_barrier_semaphore()
     for dev in (at((x + 1) % 4, y, z, c), at((x + 3) % 4, y, z, c), at(x, y, (z + 1) % 4, c),
-                at(x, y, (z + 3) % 4, c), y_dev(1), y_dev(-1), sib, partner):
+                at(x, y, (z + 3) % 4, c), y_dev(1), y_dev(-1), y_dev(2), sib, partner):
         pl.semaphore_signal(barrier, inc=1, device_id=dev, device_id_type=MESH)
-    pl.semaphore_wait(barrier, 8)
+    pl.semaphore_wait(barrier, 9)
 
     cp_sib = pltpu.make_async_remote_copy(
         src_ref=go_ref.at[:, pl.ds(pl.multiple_of((1 - c) * HALF, HALF), HALF)], dst_ref=theirs,
@@ -95,13 +99,19 @@
     cp_mine.wait()
     cp_sib.wait()
 
-    cp_hid = pltpu.make_async_remote_copy(
-        src_ref=ht.at[:, 1 - zh], dst_ref=ho, send_sem=hs.at[0], recv_sem=hr.at[0],
-        device_id=partner, device_id_type=MESH)
+    def hid_copy(t):
+        at_t = pl.ds(pl.multiple_of(t * BLK, BLK), BLK)
+        return pltpu.make_async_remote_copy(
+            src_ref=ht.at[:, 1 - zh, :, at_t], dst_ref=ho.at[:, :, at_t],
+            send_sem=hs.at[t], recv_sem=hr.at[t], device_id=partner, device_id_type=MESH)
 
     def w_copy(k, h):
         cols = pl.ds(pl.multiple_of(h * HALF + k * W, W), W)
         return pltpu.make_async_copy(w_ref.at[:, cols], wbuf.at[k % 3, h], wsem.at[k % 3, h])
+
+    def w_start(k):
+        for h in range(2):
+            w_copy(k, h).start()
 
     def e1(k):
         p, q = pq(k)
@@ -134,8 +144,6 @@
         rcopy(group(c, k, p + 1), k, 4, p_dev(k, 1)).wait_recv()
         rcopy(half(c, k, p + 1, 1), k, 6, p_dev(k, -1)).start()
         rcopy(group(c, k, p + 1), k, 9, sib).start()
-        for h in range(2):
-            w_copy(k, h).start()
 
     def e5(k):
         p, q = pq(k)
@@ -174,8 +182,12 @@
             dw += jnp.dot(ho[...].reshape(FF // 2, GROUP), rows(h, k, 1 - zh), preferred_element_type=f32)
             part[k, :, :, h * W:(h + 1) * W] = dw.astype(jnp.bfloat16).reshape(4, CHUNK, W)
         s = ysgn(k)
-        y_copy(k, blk(k, 2), ra.at[k], 12, s).start()
+        y_copy(k, blk(k, 2), ra.at[k], 12, jnp.where(k < SLICES - TAIL, s, 2)).start()
         y_copy(k, blk(k, -s), rc.at[k], 14, -s).start()
+
+        @pl.when(k >= SLICES - TAIL)
+        def _():
+            y_copy(k, blk(k, s), rb.at[k], 13, s).start()
 
     def e6b(k):
         for h in range(2):
@@ -188,10 +200,13 @@
 
     def e7(k):
         s = ysgn(k)
-        y_copy(k, blk(k, 2), ra.at[k], 12, s).wait_recv()
-        mid = (y + s + 4) % 4
-        part[k, mid] = (part[k, mid].astype(f32) + ra[k].astype(f32)).astype(jnp.bfloat16)
-        y_copy(k, blk(k, s), rb.at[k], 13, s).start()
+
+        @pl.when(k < SLICES - TAIL)
+        def _():
+            y_copy(k, blk(k, 2), ra.at[k], 12, s).wait_recv()
+            mid = (y + s + 4) % 4
+            part[k, mid] = (part[k, mid].astype(f32) + ra[k].astype(f32)).astype(jnp.bfloat16)
+            y_copy(k, blk(k, s), rb.at[k], 13, s).start()
 
     def e8(k):
         s = ysgn(k)
@@ -199,9 +214,21 @@
         y_copy(k, blk(k, s), rb.at[k], 13, s).wait_recv()
         y_copy(k, blk(k, -s), rc.at[k], 14, -s).wait_recv()
         total = part[k, y].astype(f32) + rb[k].astype(f32) + rc[k].astype(f32)
-        total = (total * scale).astype(jnp.bfloat16)
-        for h in range(2):
-            gd[:, pl.ds(pl.multiple_of(h * HALF + k * W, W), W)] = total[:, h * W:(h + 1) * W]
+
+        def put(total):
+            total = (total * scale).astype(jnp.bfloat16)
+            for h in range(2):
+                gd[:, pl.ds(pl.multiple_of(h * HALF + k * W, W), W)] = total[:, h * W:(h + 1) * W]
+
+        @pl.when(k < SLICES - TAIL)
+        def _():
+            put(total)
+
+        @pl.when(k >= SLICES - TAIL)
+        def _():
+            y_copy(k, blk(k, 2), ra.at[k], 12, 2).wait_recv()
+            put(total + ra[k].astype(f32))
+
         rcopy(one(c, k, p, q), k, 0, sib).wait_send()
         rcopy(one(c, k, p, q), k, 1, sib).wait_send()
         rcopy(one(c, k, p, q - sgn(k)), k, 2, sib).wait_send()
@@ -223,70 +250,76 @@
         gv, uv = gate[at_t, :].astype(f32), up[at_t, :].astype(f32)
         hid = (gv * jax.nn.sigmoid(gv) * uv).T.astype(jnp.bfloat16)
         ht[:, :, :, at_t] = hid.reshape(4, 2, CHUNK, BLK)
-
-    def step(i, carry):
-        def stage(off, fn):
-            k = i - off
-
-            @pl.when((k >= 0) & (k < SLICES))
-            def _():
-                fn(k)
-
-        stage(2, e3)
-        stage(1, e2)
-        stage(0, e1)
-
-        @pl.when(i == 0)
-        def _():
-            cp_gate.wait()
-            cp_up.wait()
-
-        @pl.when(i < 4)
-        def _():
-            hidden_block(2 * i)
-
-        @pl.when(i < 3)
-        def _():
-            hidden_block(2 * i + 1)
-
-        @pl.when(i == 3)
-        def _():
-            cp_hid.start()
-
-        stage(4, e4)
-        stage(5, e5)
-
-        @pl.when(i == 6)
-        def _():
-            cp_hid.wait()
-
-        stage(6, e6)
-        stage(7, e7)
-        stage(6, e6b)
-        stage(8, e8)
-        return carry
-
-    lax.fori_loop(0, SLICES + DEPTH, step, 0)
-
-    cp_gd = pltpu.make_async_copy(gd, gd_ref, osem.at[0])
-    cp_gd.start()
-
-    def finish(t, carry):
+        hid_copy(t).start()
+
+    def out_copies(t):
+        at_t = pl.ds(pl.multiple_of(t * BLK, BLK), BLK)
+        return (pltpu.make_async_copy(gate.at[at_t, :], gg_ref.at[at_t, :], osem.at[1, t]),
+                pltpu.make_async_copy(up.at[at_t, :], gu_ref.at[at_t, :], osem.at[2, t]))
+
+    def finish(t):
         at_t = pl.ds(pl.multiple_of(t * BLK, BLK), BLK)
         gv, uv, gh = gate[at_t, :].astype(f32), up[at_t, :].astype(f32), acc[at_t, :]
         sq = jax.nn.sigmoid(gv)
         gate[at_t, :] = (gh * uv * sq * (1.0 + gv * (1.0 - sq))).astype(jnp.bfloat16)
         up[at_t, :] = (gh * gv * sq).astype(jnp.bfloat16)
+        for cp in out_copies(t):
+            cp.start()
+
+    def step(i, carry):
+        def stage(off, fn):
+            k = i - off
+
+            @pl.when((k >= 0) & (k < SLICES))
+            def _():
+                fn(k)
+
+        stage(O3, e3)
+        stage(O2, e2)
+        stage(O1, e1)
+
+        @pl.when(i == 0)
+        def _():
+            cp_gate.wait()
+            cp_up.wait()
+
+        for b in range(HID_PER):
+            t = i * HID_PER + b
+
+            @pl.when(t < BLOCKS)
+            def _():
+                hidden_block(t)
+
+        stage(O4, e4)
+        stage(O5, e5)
+
+        @pl.when(i == O6)
+        def _():
+            for t in range(BLOCKS):
+                hid_copy(t).wait()
+
+        stage(O6, e6)
+        stage(O7, e7)
+        stage(O6B, e6b)
+        stage(O6 - 2, w_start)
+        stage(O8, e8)
+        for b in range(FIN_PER):
+            t = (i - (SLICES + O6B - 1)) * FIN_PER + b
+
+            @pl.when((t >= 0) & (t < BLOCKS))
+            def _():
+                finish(t)
+
         return carry
 
-    lax.fori_loop(0, GROUP // BLK, finish, 0)
-    cp_gg = pltpu.make_async_copy(gate, gg_ref, osem.at[1])
-    cp_gu = pltpu.make_async_copy(up, gu_ref, osem.at[2])
-    cp_gg.start()
-    cp_gu.start()
+    lax.fori_loop(0, SLICES + O8, step, 0)
+
+    cp_gd = pltpu.make_async_copy(gd, gd_ref, osem.at[0, 0])
+    cp_gd.start()
+    for t in range(BLOCKS):
+        for cp in out_copies(t):
+            cp.wait()
     cp_gd.wait()
-    cp_gg.wait()
-    cp_gu.wait()
 
 
 def body(grad_out, gate_act, up_act, down_weight):
@@ -316,8 +349,8 @@
             pltpu.VMEM((CHUNK // 2, HALF), bf16),
             pltpu.VMEM((CHUNK, D), bf16),
             dma((SLICES, MSGS)), dma((SLICES, MSGS)),
-            dma((1,)), dma((1,)), dma((1,)), dma((1,)),
-            dma((3, 2)), dma((3,)), dma((3,)),
+            dma((BLOCKS,)), dma((BLOCKS,)), dma((1,)), dma((1,)),
+            dma((3, 2)), dma((3,)), dma((3, BLOCKS)),
         ],
         compiler_params=pltpu.CompilerParams(
             collective_id=0, has_side_effects=True, vmem_limit_bytes=62 * 1024 * 1024),

time: 169 us -> 135 us (0.80)
  Pallas kernels: 162 us -> 128 us
    pallas_call x1, Pallas kernels: 162 us -> 128 us  [body(): pl.pallas_call(functools.partial(kernel, 1.0 / math.sqrt(token_total)), o...]
where the time goes in v2:
time: 135 us
  Pallas kernels  128 us (95%)
  local copies, waits for them, and re-layouts  6.13 us (5%)
    pallas_call x1, Pallas kernels, body(): pl.pallas_call(functools.partial(kernel, 1.0 / math.sqrt(token_total)), o...  128 us
    unnamed x7, local copies, waits for them, and re-layouts  6.13 us

profile of v2, /device:TPU:0, one launch (start us, length us, event | category | flops | bytes accessed | tf_op | source)
XLA Modules:
  0.0 134.8 jit_solution(1224900216427565576)
XLA Ops:
  0.6 128.0 %shard_map.67 = (bf16[896,896]{1,0:T(8,128)(2,1)}, bf16[896,896]{1,0:T(8,128)(2,1)}, bf16[112,8192]{1,0:T(8,128)(2,1)}) custom-call(bf16[56,8192]{1,0:T(8,128)(2,1)} %go_ref.1, bf16[896,896]{1,0:T(8,128)(2,1)} %gate_ref.1, bf16[896,896]{1,0:T(8,128)(2,1)} %up_ref.1, bf16[896,8192]{1,0:T(8,128)(2,1)} %w_ref.1), custom_call_target="tpu_custom_call" | custom-call | flops 26306674688 | bytes 25165824 | tf_op jit(solution)/shard_map/pallas_call | solution.py:330
  128.7 0.0 copy-start.1
  128.7 2.8 %copy.10 = bf16[896,896]{1,0:T(8,128)(2,1)} copy(bf16[896,896]{1,0:T(8,128)(2,1)} %get-tuple-element.6) | data formatting | bytes 3211264
  131.5 0.0 copy-done.1
  131.5 0.0 copy-start
  131.5 1.2 copy.11
  132.6 0.9 copy-done
  133.6 1.2 copy.12
Async XLA Ops:
  128.7 2.8 %copy-start.1 = (bf16[896,896]{1,0:T(8,128)(2,1)S(1)}, bf16[896,896]{1,0:T(8,128)(2,1)}, u32[]{:S(2)}) copy-start(bf16[896,896]{1,0:T(8,128)(2,1)} %get-tuple-element.7) | copy-start | bytes 4816900
  131.5 2.1 %copy-start = (bf16[112,8192]{1,0:T(8,128)(2,1)S(1)}, bf16[112,8192]{1,0:T(8,128)(2,1)}, u32[]{:S(2)}) copy-start(bf16[112,8192]{1,0:T(8,128)(2,1)} %get-tuple-element.8) | copy-start | bytes 5505028

commit v3 on v2

--- a/solution.py
+++ b/solution.py
@@ -14,15 +14,14 @@
 GROUP = 896
 CHUNK = 112
 SLICES = 16
-TAIL = 2
 W = D // 2 // SLICES
 HALF = D // 2
 MSGS = 15
 BLK = 128
 BLOCKS = GROUP // BLK
 HID_PER = 1
-FIN_PER = 3
-O1, O2, O3, O4, O5, O6, O6B, O7, O8 = 0, 2, 4, 6, 8, 9, 9, 10, 11
+FIN_PER = 2
+O1, O2, O3, O4, O5, O6, O6B, O7, O8 = 0, 2, 4, 6, 8, 9, 9, 11, 13
 
 
 def kernel(scale, go_ref, gate_ref, up_ref, w_ref, gg_ref, gu_ref, gd_ref,
@@ -87,9 +86,9 @@
 
     barrier = pltpu.get_barrier_semaphore()
     for dev in (at((x + 1) % 4, y, z, c), at((x + 3) % 4, y, z, c), at(x, y, (z + 1) % 4, c),
-                at(x, y, (z + 3) % 4, c), y_dev(1), y_dev(-1), y_dev(2), sib, partner):
+                at(x, y, (z + 3) % 4, c), y_dev(1), y_dev(-1), sib, partner):
         pl.semaphore_signal(barrier, inc=1, device_id=dev, device_id_type=MESH)
-    pl.semaphore_wait(barrier, 9)
+    pl.semaphore_wait(barrier, 8)
 
     cp_sib = pltpu.make_async_remote_copy(
         src_ref=go_ref.at[:, pl.ds(pl.multiple_of((1 - c) * HALF, HALF), HALF)], dst_ref=theirs,
@@ -182,12 +181,8 @@
             dw += jnp.dot(ho[...].reshape(FF // 2, GROUP), rows(h, k, 1 - zh), preferred_element_type=f32)
             part[k, :, :, h * W:(h + 1) * W] = dw.astype(jnp.bfloat16).reshape(4, CHUNK, W)
         s = ysgn(k)
-        y_copy(k, blk(k, 2), ra.at[k], 12, jnp.where(k < SLICES - TAIL, s, 2)).start()
+        y_copy(k, blk(k, 2), ra.at[k], 12, s).start()
         y_copy(k, blk(k, -s), rc.at[k], 14, -s).start()
-
-        @pl.when(k >= SLICES - TAIL)
-        def _():
-            y_copy(k, blk(k, s), rb.at[k], 13, s).start()
 
     def e6b(k):
         for h in range(2):
@@ -200,13 +195,10 @@
 
     def e7(k):
         s = ysgn(k)
-
-        @pl.when(k < SLICES - TAIL)
-        def _():
-            y_copy(k, blk(k, 2), ra.at[k], 12, s).wait_recv()
-            mid = (y + s + 4) % 4
-            part[k, mid] = (part[k, mid].astype(f32) + ra[k].astype(f32)).astype(jnp.bfloat16)
-            y_copy(k, blk(k, s), rb.at[k], 13, s).start()
+        y_copy(k, blk(k, 2), ra.at[k], 12, s).wait_recv()
+        mid = (y + s + 4) % 4
+        part[k, mid] = (part[k, mid].astype(f32) + ra[k].astype(f32)).astype(jnp.bfloat16)
+        y_copy(k, blk(k, s), rb.at[k], 13, s).start()
 
     def e8(k):
         s = ysgn(k)
@@ -214,21 +206,9 @@
         y_copy(k, blk(k, s), rb.at[k], 13, s).wait_recv()
         y_copy(k, blk(k, -s), rc.at[k], 14, -s).wait_recv()
         total = part[k, y].astype(f32) + rb[k].astype(f32) + rc[k].astype(f32)
-
-        def put(total):
-            total = (total * scale).astype(jnp.bfloat16)
-            for h in range(2):
-                gd[:, pl.ds(pl.multiple_of(h * HALF + k * W, W), W)] = total[:, h * W:(h + 1) * W]
-
-        @pl.when(k < SLICES - TAIL)
-        def _():
-            put(total)
-
-        @pl.when(k >= SLICES - TAIL)
-        def _():
-            y_copy(k, blk(k, 2), ra.at[k], 12, 2).wait_recv()
-            put(total + ra[k].astype(f32))
-
+        total = (total * scale).astype(jnp.bfloat16)
+        for h in range(2):
+            gd[:, pl.ds(pl.multiple_of(h * HALF + k * W, W), W)] = total[:, h * W:(h + 1) * W]
         rcopy(one(c, k, p, q), k, 0, sib).wait_send()
         rcopy(one(c, k, p, q), k, 1, sib).wait_send()
         rcopy(one(c, k, p, q - sgn(k)), k, 2, sib).wait_send()
@@ -274,9 +254,9 @@
             def _():
                 fn(k)
 
-        stage(O3, e3)
         stage(O2, e2)
         stage(O1, e1)
+        stage(O3, e3)
 
         @pl.when(i == 0)
         def _():

time: 135 us -> 133 us (0.985)
  Pallas kernels: 128 us -> 126 us
    pallas_call x1, Pallas kernels: 128 us -> 126 us  [body(): pl.pallas_call(functools.partial(kernel, 1.0 / math.sqrt(token_total)), o...]
where the time goes in v3:
time: 133 us
  Pallas kernels  126 us (95%)
  local copies, waits for them, and re-layouts  6.13 us (5%)
    pallas_call x1, Pallas kernels, body(): pl.pallas_call(functools.partial(kernel, 1.0 / math.sqrt(token_total)), o...  126 us
    unnamed x7, local copies, waits for them, and re-layouts  6.13 us

profile of v3, /device:TPU:0, one launch (start us, length us, event | category | flops | bytes accessed | tf_op | source)
XLA Modules:
  0.0 133.2 jit_solution(15617050461902023783)
XLA Ops:
  0.6 126.5 %shard_map.67 = (bf16[896,896]{1,0:T(8,128)(2,1)}, bf16[896,896]{1,0:T(8,128)(2,1)}, bf16[112,8192]{1,0:T(8,128)(2,1)}) custom-call(bf16[56,8192]{1,0:T(8,128)(2,1)} %go_ref.1, bf16[896,896]{1,0:T(8,128)(2,1)} %gate_ref.1, bf16[896,896]{1,0:T(8,128)(2,1)} %up_ref.1, bf16[896,8192]{1,0:T(8,128)(2,1)} %w_ref.1), custom_call_target="tpu_custom_call" | custom-call | flops 26306674688 | bytes 25165824 | tf_op jit(solution)/shard_map/pallas_call | solution.py:310
  127.1 0.0 copy-start.1
  127.1 2.8 %copy.10 = bf16[896,896]{1,0:T(8,128)(2,1)} copy(bf16[896,896]{1,0:T(8,128)(2,1)} %get-tuple-element.6) | data formatting | bytes 3211264
  129.9 0.0 copy-done.1
  129.9 0.0 copy-start
  129.9 1.2 copy.11
  131.1 0.9 copy-done
  132.0 1.2 copy.12
Async XLA Ops:
  127.1 2.8 %copy-start.1 = (bf16[896,896]{1,0:T(8,128)(2,1)S(1)}, bf16[896,896]{1,0:T(8,128)(2,1)}, u32[]{:S(2)}) copy-start(bf16[896,896]{1,0:T(8,128)(2,1)} %get-tuple-element.7) | copy-start | bytes 4816900
  129.9 2.1 %copy-start = (bf16[112,8192]{1,0:T(8,128)(2,1)S(1)}, bf16[112,8192]{1,0:T(8,128)(2,1)}, u32[]{:S(2)}) copy-start(bf16[112,8192]{1,0:T(8,128)(2,1)} %get-tuple-element.8) | copy-start | bytes 5505028

commit v4 on v3

--- a/solution.py
+++ b/solution.py
@@ -20,13 +20,14 @@
 BLK = 128
 BLOCKS = GROUP // BLK
 HID_PER = 1
+PIECES = 4
 FIN_PER = 2
 O1, O2, O3, O4, O5, O6, O6B, O7, O8 = 0, 2, 4, 6, 8, 9, 9, 11, 13
 
 
 def kernel(scale, go_ref, gate_ref, up_ref, w_ref, gg_ref, gu_ref, gd_ref,
            g, ht, ho, gate, up, acc, wbuf, part, ra, rb, rc, mine, theirs, gd,
-           ss, rs, hs, hr, ls, lr, wsem, lsem, osem):
+           ss, rs, hs, hr, ls, lr, wsem, lsem, osem, gsem):
     tp, dp = lax.axis_index("tp"), lax.axis_index("dp")
     x, y, c = tp // 4, dp // 2, tp % 2
     zh, zl = dp % 2, (tp // 2) % 2
@@ -79,8 +80,20 @@
 
     cp_gate = pltpu.make_async_copy(gate_ref, gate, lsem.at[0])
     cp_up = pltpu.make_async_copy(up_ref, up, lsem.at[1])
-    cp_mine = pltpu.make_async_copy(go_ref.at[:, pl.ds(pl.multiple_of(c * HALF, HALF), HALF)], mine, lsem.at[2])
-    cp_mine.start()
+    part_w = HALF // PIECES
+
+    def mine_copy(n):
+        src = go_ref.at[:, pl.ds(pl.multiple_of(c * HALF + n * part_w, part_w), part_w)]
+        return pltpu.make_async_copy(src, mine.at[:, pl.ds(pl.multiple_of(n * part_w, part_w), part_w)], lsem.at[2 + n])
+
+    def theirs_copy(n):
+        src = go_ref.at[:, pl.ds(pl.multiple_of((1 - c) * HALF + n * part_w, part_w), part_w)]
+        return pltpu.make_async_remote_copy(
+            src_ref=src, dst_ref=theirs.at[:, pl.ds(pl.multiple_of(n * part_w, part_w), part_w)],
+            send_sem=ls.at[n], recv_sem=lr.at[n], device_id=sib, device_id_type=MESH)
+
+    for n in range(PIECES):
+        mine_copy(n).start()
     cp_gate.start()
     cp_up.start()
 
@@ -90,13 +103,9 @@
         pl.semaphore_signal(barrier, inc=1, device_id=dev, device_id_type=MESH)
     pl.semaphore_wait(barrier, 8)
 
-    cp_sib = pltpu.make_async_remote_copy(
-        src_ref=go_ref.at[:, pl.ds(pl.multiple_of((1 - c) * HALF, HALF), HALF)], dst_ref=theirs,
-        send_sem=ls.at[0], recv_sem=lr.at[0], device_id=sib, device_id_type=MESH)
-    cp_sib.start()
+    for n in range(PIECES):
+        theirs_copy(n).start()
     acc[...] = jnp.zeros_like(acc)
-    cp_mine.wait()
-    cp_sib.wait()
 
     def hid_copy(t):
         at_t = pl.ds(pl.multiple_of(t * BLK, BLK), BLK)
@@ -114,6 +123,13 @@
 
     def e1(k):
         p, q = pq(k)
+
+        @pl.when(k % (SLICES // PIECES) == 0)
+        def _():
+            n = k // (SLICES // PIECES)
+            mine_copy(n).wait()
+            theirs_copy(n).wait()
+
         cols = pl.ds(pl.multiple_of(k * W, W), W)
         a, b = mine[:, cols], theirs[:, cols]
         first, last = jnp.where(c == 0, a, b), jnp.where(c == 0, b, a)
@@ -200,6 +216,10 @@
         part[k, mid] = (part[k, mid].astype(f32) + ra[k].astype(f32)).astype(jnp.bfloat16)
         y_copy(k, blk(k, s), rb.at[k], 13, s).start()
 
+    def gd_copy(k, h):
+        cols = pl.ds(pl.multiple_of(h * HALF + k * W, W), W)
+        return pltpu.make_async_copy(gd.at[:, cols], gd_ref.at[:, cols], gsem.at[k, h])
+
     def e8(k):
         s = ysgn(k)
         p, q = pq(k)
@@ -209,6 +229,7 @@
         total = (total * scale).astype(jnp.bfloat16)
         for h in range(2):
             gd[:, pl.ds(pl.multiple_of(h * HALF + k * W, W), W)] = total[:, h * W:(h + 1) * W]
+            gd_copy(k, h).start()
         rcopy(one(c, k, p, q), k, 0, sib).wait_send()
         rcopy(one(c, k, p, q), k, 1, sib).wait_send()
         rcopy(one(c, k, p, q - sgn(k)), k, 2, sib).wait_send()
@@ -294,12 +315,15 @@
 
     lax.fori_loop(0, SLICES + O8, step, 0)
 
-    cp_gd = pltpu.make_async_copy(gd, gd_ref, osem.at[0, 0])
-    cp_gd.start()
+    def gd_wait(k, carry):
+        for h in range(2):
+            gd_copy(k, h).wait()
+        return carry
+
+    lax.fori_loop(0, SLICES, gd_wait, 0)
     for t in range(BLOCKS):
         for cp in out_copies(t):
             cp.wait()
-    cp_gd.wait()
 
 
 def body(grad_out, gate_act, up_act, down_weight):
@@ -329,8 +353,8 @@
             pltpu.VMEM((CHUNK // 2, HALF), bf16),
             pltpu.VMEM((CHUNK, D), bf16),
             dma((SLICES, MSGS)), dma((SLICES, MSGS)),
-            dma((BLOCKS,)), dma((BLOCKS,)), dma((1,)), dma((1,)),
-            dma((3, 2)), dma((3,)), dma((3, BLOCKS)),
+            dma((BLOCKS,)), dma((BLOCKS,)), dma((PIECES,)), dma((PIECES,)),
+            dma((3, 2)), dma((2 + PIECES,)), dma((3, BLOCKS)), dma((SLICES, 2)),
         ],
         compiler_params=pltpu.CompilerParams(
             collective_id=0, has_side_effects=True, vmem_limit_bytes=62 * 1024 * 1024),

time: 133 us -> 133 us (level)
  no operation moved by 1% of the time
where the time goes in v4:
time: 133 us
  Pallas kernels  126 us (95%)
  local copies, waits for them, and re-layouts  6.13 us (5%)
    pallas_call x1, Pallas kernels, body(): pl.pallas_call(functools.partial(kernel, 1.0 / math.sqrt(token_total)), o...  126 us
    unnamed x7, local copies, waits for them, and re-layouts  6.13 us

profile of v4, /device:TPU:0, one launch (start us, length us, event | category | flops | bytes accessed | tf_op | source)
XLA Modules:
  0.0 132.5 jit_solution(2180342990972772513)
XLA Ops:
  0.6 125.7 %shard_map.67 = (bf16[896,896]{1,0:T(8,128)(2,1)}, bf16[896,896]{1,0:T(8,128)(2,1)}, bf16[112,8192]{1,0:T(8,128)(2,1)}) custom-call(bf16[56,8192]{1,0:T(8,128)(2,1)} %go_ref.1, bf16[896,896]{1,0:T(8,128)(2,1)} %gate_ref.1, bf16[896,896]{1,0:T(8,128)(2,1)} %up_ref.1, bf16[896,8192]{1,0:T(8,128)(2,1)} %w_ref.1), custom_call_target="tpu_custom_call" | custom-call | flops 26306674688 | bytes 25165824 | tf_op jit(solution)/shard_map/pallas_call | solution.py:334
  126.4 0.0 copy-start.1
  126.4 2.8 %copy.10 = bf16[896,896]{1,0:T(8,128)(2,1)} copy(bf16[896,896]{1,0:T(8,128)(2,1)} %get-tuple-element.6) | data formatting | bytes 3211264
  129.2 0.0 copy-done.1
  129.2 0.0 copy-start
  129.2 1.2 copy.11
  130.4 0.9 copy-done
  131.3 1.2 copy.12
Async XLA Ops:
  126.4 2.8 %copy-start.1 = (bf16[896,896]{1,0:T(8,128)(2,1)S(1)}, bf16[896,896]{1,0:T(8,128)(2,1)}, u32[]{:S(2)}) copy-start(bf16[896,896]{1,0:T(8,128)(2,1)} %get-tuple-element.7) | copy-start | bytes 4816900
  129.2 2.1 %copy-start = (bf16[112,8192]{1,0:T(8,128)(2,1)S(1)}, bf16[112,8192]{1,0:T(8,128)(2,1)}, u32[]{:S(2)}) copy-start(bf16[112,8192]{1,0:T(8,128)(2,1)} %get-tuple-element.8) | copy-start | bytes 5505028

commit v5 on v4

--- a/solution.py
+++ b/solution.py
@@ -20,7 +20,7 @@
 BLK = 128
 BLOCKS = GROUP // BLK
 HID_PER = 1
-PIECES = 4
+PIECES = 8
 FIN_PER = 2
 O1, O2, O3, O4, O5, O6, O6B, O7, O8 = 0, 2, 4, 6, 8, 9, 9, 11, 13
 
@@ -301,9 +301,9 @@
 
         stage(O6, e6)
         stage(O7, e7)
-        stage(O6B, e6b)
         stage(O6 - 2, w_start)
         stage(O8, e8)
+        stage(O6B, e6b)
         for b in range(FIN_PER):
             t = (i - (SLICES + O6B - 1)) * FIN_PER + b
 

time: 133 us -> 133 us (level)
  no operation moved by 1% of the time
where the time goes in v5:
time: 133 us
  Pallas kernels  126 us (95%)
  local copies, waits for them, and re-layouts  6.13 us (5%)
    pallas_call x1, Pallas kernels, body(): pl.pallas_call(functools.partial(kernel, 1.0 / math.sqrt(token_total)), o...  126 us
    unnamed x7, local copies, waits for them, and re-layouts  6.13 us

profile of v5, /device:TPU:0, one launch (start us, length us, event | category | flops | bytes accessed | tf_op | source)
XLA Modules:
  0.0 132.5 jit_solution(1373656398865867678)
XLA Ops:
  0.6 125.8 %shard_map.67 = (bf16[896,896]{1,0:T(8,128)(2,1)}, bf16[896,896]{1,0:T(8,128)(2,1)}, bf16[112,8192]{1,0:T(8,128)(2,1)}) custom-call(bf16[56,8192]{1,0:T(8,128)(2,1)} %go_ref.1, bf16[896,896]{1,0:T(8,128)(2,1)} %gate_ref.1, bf16[896,896]{1,0:T(8,128)(2,1)} %up_ref.1, bf16[896,8192]{1,0:T(8,128)(2,1)} %w_ref.1), custom_call_target="tpu_custom_call" | custom-call | flops 26306674688 | bytes 25165824 | tf_op jit(solution)/shard_map/pallas_call | solution.py:334
  126.4 0.0 copy-start.1
  126.4 2.8 %copy.10 = bf16[896,896]{1,0:T(8,128)(2,1)} copy(bf16[896,896]{1,0:T(8,128)(2,1)} %get-tuple-element.6) | data formatting | bytes 3211264
  129.2 0.0 copy-done.1
  129.2 0.0 copy-start
  129.2 1.2 copy.11
  130.4 0.9 copy-done
  131.3 1.2 copy.12
Async XLA Ops:
  126.4 2.8 %copy-start.1 = (bf16[896,896]{1,0:T(8,128)(2,1)S(1)}, bf16[896,896]{1,0:T(8,128)(2,1)}, u32[]{:S(2)}) copy-start(bf16[896,896]{1,0:T(8,128)(2,1)} %get-tuple-element.7) | copy-start | bytes 4816900
  129.2 2.1 %copy-start = (bf16[112,8192]{1,0:T(8,128)(2,1)S(1)}, bf16[112,8192]{1,0:T(8,128)(2,1)}, u32[]{:S(2)}) copy-start(bf16[112,8192]{1,0:T(8,128)(2,1)} %get-tuple-element.8) | copy-start | bytes 5505028
